TPU v7x, 32 devices: a whole 2x2x4 slice. The times are simulated.
32 devices in a mesh: ctx: 16 (over z, y, x), head: 2 (over core).
Axes of the slice: x: 2, y: 2, z: 4, core: 2. Of those that a mesh axis runs over, the one named last changes fastest.
Arguments:
- queries: bfloat16 [6144, 4096], P('ctx', 'head'), may hold values from -200 to 200
- key_matrix: bfloat16 [6144, 1024], P('ctx', 'head'), may hold values from -6 to 6
- value_matrix: bfloat16 [6144, 1024], P('ctx', 'head'), may hold values from -6 to 6
- doc_ids: int32 [6144], P('ctx'), may hold values from 0 to 7, never falling along the last dimension, each value on 1 to 3456 neighbouring positions
- out_weight: bfloat16 [4096, 4096], P('head'), may hold values from -0.09375 to 0.09375
Outputs:
- projected: bfloat16 [6144, 4096], P(('ctx', 'head'))
Inputs may be any that keep to these rules, and one draw needn't show every extreme that they name: `doc_ids`: document ids never fall along the tokens; each document has 1 to 3456 tokens and one has exactly 3456.
All inputs are finite; a program needn't handle non-finite values.
Results may differ from a plain program's by a relative error of at most 0.019.
Values may be sent and summed in bfloat16 or wider, within the bound.
A program may use at most 256 MiB of HBM per device.

v0:
```python
import functools
import jax
import jax.numpy as jnp
from jax import lax
from jax.experimental import pallas as pl
from jax.experimental.pallas import tpu as pltpu
from jax.sharding import PartitionSpec as P

HEAD_WIDTH = 128


def gathered_attention(queries, key_matrix, value_matrix, doc_ids, out_weight):
    tok_rows = queries.shape[0]
    kv_here = key_matrix.shape[1] // HEAD_WIDTH
    queries_per_group = queries.shape[1] // key_matrix.shape[1]
    all_rows = queries_per_group * tok_rows
    my_index = lax.axis_index("ctx")
    q_pos = my_index * tok_rows + jnp.arange(tok_rows, dtype=jnp.int32)
    q_rows = (
        queries.reshape(tok_rows, kv_here, queries_per_group, HEAD_WIDTH)
        .transpose(1, 2, 0, 3)
        .reshape(kv_here, all_rows, HEAD_WIDTH)
    )
    score_scale = HEAD_WIDTH ** (-0.5)
    running = jnp.full((kv_here, all_rows), -1e30, jnp.float32)
    part_keys = lax.all_gather(key_matrix, "ctx", axis=0, tiled=True)
    part_values = lax.all_gather(value_matrix, "ctx", axis=0, tiled=True)
    part_docs = lax.all_gather(doc_ids, "ctx", axis=0, tiled=True)
    key_count = part_keys.shape[0]
    k_pos = jnp.arange(key_count, dtype=jnp.int32)
    keys_three = part_keys.reshape(key_count, kv_here, HEAD_WIDTH).transpose(1, 0, 2)
    values_three = part_values.reshape(key_count, kv_here, HEAD_WIDTH).transpose(1, 0, 2)
    scores = (
        jnp.einsum("hqd,hkd->hqk", q_rows, keys_three, preferred_element_type=jnp.float32)
        * score_scale
    )
    allowed = (
        (doc_ids[:, None] == part_docs[None, :])
        & (q_pos[:, None] >= k_pos[None, :])
        & (k_pos[None, :] >= 0)
    )
    allowed = jnp.tile(allowed, (queries_per_group, 1))[None]
    scores = jnp.where(allowed, scores, jnp.float32(-1e30))
    new_max = jnp.maximum(running, jnp.max(scores, axis=-1))
    weights = jnp.where(allowed, jnp.exp(scores - new_max[..., None]), jnp.float32(0.0))
    denominator = jnp.sum(weights, axis=-1)
    weighted = jnp.einsum(
        "hqk,hkd->hqd",
        weights.astype(jnp.bfloat16),
        values_three,
        preferred_element_type=jnp.float32,
    )
    running_state = (new_max, denominator, weighted)
    running, denominator, weighted = running_state
    attended = (weighted / denominator[..., None]).astype(jnp.bfloat16)
    attended = (
        attended.reshape(kv_here, queries_per_group, tok_rows, HEAD_WIDTH)
        .transpose(2, 0, 1, 3)
        .reshape(tok_rows, kv_here * queries_per_group * HEAD_WIDTH)
    )
    return lax.psum_scatter(
        jnp.dot(attended, out_weight, preferred_element_type=jnp.float32).astype(jnp.bfloat16),
        "head",
        scatter_dimension=0,
        tiled=True,
    )


NEG = -1e30
LOG2E = 1.4426950408889634
PLANE = 4
REACH = 9
SLOTS = REACH + 1
OUT_TILE = 512


def fused_kernel(
    q_ref, k_ref, v_ref, doc_ref, w_hbm, out_ref,
    kv, docs, q_wide, k_wide, v_wide, m_s, acc, att, w_vm, part, theirs, swapped,
    send_sem, recv_sem, dsend_sem, drecv_sem, w_sem, osend_sem, orecv_sem,
):
    tok = q_ref.shape[0]
    heads = k_ref.shape[1] // HEAD_WIDTH
    group = q_ref.shape[1] // k_ref.shape[1]
    me = lax.axis_index("ctx")
    core = lax.axis_index("head")
    z, y, x = me // PLANE, (me // 2) % 2, me % 2
    dx, dy = 1 - 2 * x, 2 - 4 * y
    x_src = (4 * x, 4 + 4 * x, 2 + 4 * (1 - x) * (1 - y))
    y_src = (4 * y, 4 + 4 * y, 3 + 4 * y + x * (2 - 4 * y))
    z_src = (0, 4, 5)
    planes = lax.axis_size("ctx") // PLANE
    links = (
        (x_src, dx, None),
        (y_src, dy, None),
        (z_src, PLANE, z < planes - 1),
    )

    barrier = pltpu.get_barrier_semaphore()
    pl.semaphore_signal(barrier, inc=1, device_id={"ctx": me + dx})
    pl.semaphore_signal(barrier, inc=1, device_id={"ctx": me + dy})
    pl.semaphore_signal(barrier, inc=1, device_id={"head": 1 - core})

    @pl.when(z < planes - 1)
    def _():
        pl.semaphore_signal(barrier, inc=1, device_id={"ctx": me + PLANE})

    @pl.when(z > 0)
    def _():
        pl.semaphore_signal(barrier, inc=1, device_id={"ctx": me - PLANE})

    weight_copy = pltpu.make_async_copy(w_hbm, w_vm, w_sem)
    weight_copy.start()
    for h in range(heads):
        columns = pl.ds(h * HEAD_WIDTH, HEAD_WIDTH)
        kv[0, h, 0] = k_ref[:, columns]
        kv[0, h, 1] = v_ref[:, columns]
    docs[0] = jnp.broadcast_to(doc_ref[...], docs.shape[1:])

    def blank(s, carry):
        docs[s] = jnp.full(docs.shape[1:], -1, jnp.int32)
        kv[s] = jnp.zeros(kv.shape[1:], kv.dtype)
        return carry

    lax.fori_loop(jnp.minimum(me + 1, SLOTS), SLOTS, blank, 0)

    peers = 3 + jnp.where(z > 0, 1, 0) + jnp.where(z < planes - 1, 1, 0)
    pl.semaphore_wait(barrier, peers)

    def chunk_copy(link, s, h):
        step = links[link][1]
        return pltpu.make_async_remote_copy(
            src_ref=kv.at[s, h],
            dst_ref=kv.at[s + step, h],
            send_sem=send_sem.at[link, s, h],
            recv_sem=recv_sem.at[s + step, h],
            device_id={"ctx": me + step},
        )

    def doc_copy(link, s):
        step = links[link][1]
        return pltpu.make_async_remote_copy(
            src_ref=docs.at[s],
            dst_ref=docs.at[s + step],
            send_sem=dsend_sem.at[link, s],
            recv_sem=drecv_sem.at[s + step],
            device_id={"ctx": me + step},
        )

    def sends(link, s):
        sources, _, also = links[link]
        here = (s == sources[0]) | (s == sources[1]) | (s == sources[2])
        if also is not None:
            here = here & also
        return here

    def forward(s, h):
        for link in (2, 0, 1):
            @pl.when(sends(link, s))
            def _():
                @pl.when(h == 0)
                def _():
                    doc_copy(link, s).start()

                chunk_copy(link, s, h).start()

    def send_own(h, carry):
        forward(jnp.int32(0), h)
        return carry

    lax.fori_loop(0, heads, send_own, 0)

    score_scale = HEAD_WIDTH ** (-0.5) * LOG2E
    doc_rows = lax.broadcasted_iota(jnp.int32, (HEAD_WIDTH, tok), 0)

    def doc_columns(s, same, other):
        flags = jnp.where(docs[s, 0:1, :] == doc_rows, same, other).astype(jnp.float32)
        return flags.T.astype(jnp.bfloat16)

    own_docs = doc_columns(0, 1.0, 0.0)
    for head in range(heads * group):
        q_wide[head, :, :HEAD_WIDTH] = q_ref[:, head * HEAD_WIDTH:(head + 1) * HEAD_WIDTH]
        q_wide[head, :, HEAD_WIDTH:] = own_docs
    v_wide[:, HEAD_WIDTH:] = jnp.ones((v_wide.shape[0], HEAD_WIDTH), jnp.bfloat16)

    def fill(j, s, h):
        k_wide[j * tok:(j + 1) * tok, :HEAD_WIDTH] = kv[s, h, 0]
        v_wide[j * tok:(j + 1) * tok, :HEAD_WIDTH] = kv[s, h, 1]

        @pl.when(h == 0)
        def _():
            k_wide[j * tok:(j + 1) * tok, HEAD_WIDTH:] = doc_columns(s, 0.0, NEG)

    def piece(h, count, first):
        keys = k_wide[:count]
        values = v_wide[:count]

        def score(r):
            return lax.dot_general(
                q_wide[h * group + r], keys, (((1,), (1,)), ((), ())),
                preferred_element_type=jnp.float32,
            )

        upcoming = score(0)
        for r in range(group):
            scores = upcoming
            if r + 1 < group:
                upcoming = score(r + 1)
            head = h * group + r
            if first:
                rows = lax.broadcasted_iota(jnp.int32, (tok, tok), 0)
                cols = lax.broadcasted_iota(jnp.int32, (tok, tok), 1)
                scores = jnp.where(rows >= cols, scores, NEG)
            top = jnp.broadcast_to(
                jnp.max(scores, axis=1, keepdims=True), (tok, HEAD_WIDTH)
            )
            if not first:
                before = m_s[head]
                top = jnp.maximum(before, top)
            shift = jnp.concatenate([top * score_scale] * (count // HEAD_WIDTH), axis=1)
            weights = jnp.exp2(scores * score_scale - shift).astype(jnp.bfloat16)
            summed = jnp.dot(weights, values, preferred_element_type=jnp.float32)
            if not first:
                fade = jnp.exp2((before - top) * score_scale)
                summed = summed + acc[head] * jnp.concatenate([fade, fade], axis=1)
            m_s[head] = top
            acc[head] = summed

    def own_piece(h, carry):
        fill(0, 0, h)
        piece(h, tok, True)
        return carry

    lax.fori_loop(0, heads, own_piece, 0)

    turn = 3
    x_third = x * (7 - 4 * y) + (1 - x)
    y_third = x * (3 + 4 * y) + (1 - x) * 5

    def pick(place):
        z_slot = jnp.where(place < turn, 4, jnp.where(place < 2 * turn, 8, REACH))
        x_slot = jnp.where(place < turn, 3 - 2 * x, jnp.where(place < 2 * turn, 7 - 2 * x, x_third))
        y_slot = jnp.where(place < turn, 2, jnp.where(place < 2 * turn, 6, y_third))
        j = place % turn
        late = place >= 2 * turn
        first = jnp.where(late, x_slot, z_slot)
        second = jnp.where(late, y_slot, x_slot)
        third = jnp.where(late, z_slot, y_slot)
        return jnp.where(j == 0, first, jnp.where(j == 1, second, third))

    def arrive(t, carry):
        around = t // heads
        h = t % heads
        for j in range(turn):
            s = pick(around * turn + j)

            @pl.when(me >= s)
            def _():
                pltpu.make_async_copy(kv.at[s, h], kv.at[s, h], recv_sem.at[s, h]).wait()

                @pl.when(h == 0)
                def _():
                    pltpu.make_async_copy(docs.at[s], docs.at[s], drecv_sem.at[s]).wait()

                forward(s, h)

        for j in range(turn):
            fill(j, pick(around * turn + j), h)
        piece(h, turn * tok, False)
        return carry

    lax.fori_loop(0, REACH // turn * heads, arrive, 0)

    def finish(head, carry):
        att[:, pl.ds(pl.multiple_of(head * HEAD_WIDTH, HEAD_WIDTH), HEAD_WIDTH)] = (
            acc[head, :, :HEAD_WIDTH] / acc[head, :, HEAD_WIDTH:]
        ).astype(jnp.bfloat16)
        return carry

    lax.fori_loop(0, heads * group, finish, 0)
    weight_copy.wait()

    half = out_ref.shape[0]
    tiles = out_ref.shape[1] // OUT_TILE
    keep = pl.multiple_of(core * half, half)
    give = pl.multiple_of((1 - core) * half, half)

    def swap_copy(i):
        return pltpu.make_async_remote_copy(
            src_ref=theirs.at[i],
            dst_ref=swapped.at[i],
            send_sem=osend_sem.at[i],
            recv_sem=orecv_sem.at[i],
            device_id={"head": 1 - core},
        )

    def project(i, carry):
        columns = pl.ds(pl.multiple_of(i * OUT_TILE, OUT_TILE), OUT_TILE)
        part[...] = jnp.dot(att[...], w_vm[:, columns], preferred_element_type=jnp.float32)
        theirs[i] = part[pl.ds(give, half), :].astype(jnp.bfloat16)
        swap_copy(i).start()
        out_ref[:, columns] = part[pl.ds(keep, half), :].astype(jnp.bfloat16)
        return carry

    lax.fori_loop(0, tiles, project, 0)

    def combine(i, carry):
        swap_copy(i).wait()
        columns = pl.ds(pl.multiple_of(i * OUT_TILE, OUT_TILE), OUT_TILE)
        out_ref[:, columns] = (
            out_ref[:, columns].astype(jnp.float32) + swapped[i].astype(jnp.float32)
        ).astype(jnp.bfloat16)
        return carry

    lax.fori_loop(0, tiles, combine, 0)

    def settle(s, carry):
        for link in range(3):
            @pl.when(sends(link, s) & (me >= s))
            def _():
                doc_copy(link, s).wait_send()
                for h in range(heads):
                    chunk_copy(link, s, h).wait_send()
        return carry

    lax.fori_loop(0, SLOTS, settle, 0)


def fused_device(queries, key_matrix, value_matrix, doc_ids, out_weight):
    tok, width = queries.shape
    heads = key_matrix.shape[1] // HEAD_WIDTH
    query_heads = width // HEAD_WIDTH
    out_width = out_weight.shape[1]
    half = tok // 2
    tiles = out_width // OUT_TILE
    vmem = pl.BlockSpec(memory_space=pltpu.VMEM)
    f32, bf16 = jnp.float32, jnp.bfloat16
    return pl.pallas_call(
        fused_kernel,
        out_shape=jax.ShapeDtypeStruct((half, out_width), bf16),
        in_specs=[vmem] * 4 + [pl.BlockSpec(memory_space=pl.ANY)],
        out_specs=vmem,
        scratch_shapes=[
            pltpu.VMEM((SLOTS, heads, 2, tok, HEAD_WIDTH), bf16),
            pltpu.VMEM((SLOTS, 8, tok), jnp.int32),
            pltpu.VMEM((query_heads, tok, 2 * HEAD_WIDTH), bf16),
            pltpu.VMEM((3 * tok, 2 * HEAD_WIDTH), bf16),
            pltpu.VMEM((3 * tok, 2 * HEAD_WIDTH), bf16),
            pltpu.VMEM((query_heads, tok, HEAD_WIDTH), f32),
            pltpu.VMEM((query_heads, tok, 2 * HEAD_WIDTH), f32),
            pltpu.VMEM((tok, width), bf16),
            pltpu.VMEM(out_weight.shape, bf16),
            pltpu.VMEM((tok, OUT_TILE), f32),
            pltpu.VMEM((tiles, half, OUT_TILE), bf16),
            pltpu.VMEM((tiles, half, OUT_TILE), bf16),
            pltpu.SemaphoreType.DMA((3, SLOTS, heads)),
            pltpu.SemaphoreType.DMA((SLOTS, heads)),
            pltpu.SemaphoreType.DMA((3, SLOTS)),
            pltpu.SemaphoreType.DMA((SLOTS,)),
            pltpu.SemaphoreType.DMA,
            pltpu.SemaphoreType.DMA((tiles,)),
            pltpu.SemaphoreType.DMA((tiles,)),
        ],
        compiler_params=pltpu.CompilerParams(
            collective_id=0, has_side_effects=True, vmem_limit_bytes=58 * 1024 * 1024
        ),
    )(queries, key_matrix, value_matrix, doc_ids[None, :], out_weight)


def solution(mesh):
    placed = (P("ctx", "head"), P("ctx", "head"), P("ctx", "head"), P("ctx"), P("head", None))
    neighbours = mesh.shape["ctx"] == 4 * PLANE and mesh.shape["head"] == 2
    return jax.shard_map(
        fused_device if neighbours else gathered_attention,
        mesh=mesh,
        in_specs=placed,
        out_specs=P(("ctx", "head"), None),
        check_vma=False,
    )
```

profile of v0, /device:TPU:25, one launch (start us, length us, event | category | flops | bytes accessed | tf_op | source)
XLA Modules:
  0.0 119.8 jit_solution(17761299256700014364)
XLA Ops:
  0.0 1.2 %broadcast_in_dim.3.doc_ref = s32[1,384]{1,0:T(1,128)} reshape(s32[384]{0:T(512)} %param.8) | data formatting | bytes 3072 | tf_op jit(solution)/shard_map/broadcast_in_dim | solution.py:367
  1.2 115.9 %shard_map.55 = bf16[192,4096]{1,0:T(8,128)(2,1)} custom-call(bf16[384,2048]{1,0:T(8,128)(2,1)} %q_ref.1, bf16[384,512]{1,0:T(8,128)(2,1)} %k_ref.1, bf16[384,512]{1,0:T(8,128)(2,1)} %v_ref.1, s32[1,384]{1,0:T(1,128)} %broadcast_in_dim.3.doc_ref, bf16[2048,4096]{1,0:T(8,128)(2,1)} %w_hbm.1), custom_call_target="tpu_custom_call" | custom-call | tf_op jit(solution)/shard_map/pallas_call | solution.py:338
  117.1 2.7 %copy.7 = bf16[192,4096]{1,0:T(8,128)(2,1)} copy(bf16[192,4096]{1,0:T(8,128)(2,1)} %shard_map.55) | data formatting | bytes 3145728
where the time goes:
time: 120 us
  Pallas kernels  116 us (97%)
  local copies, waits for them, and re-layouts  3.95 us (3%)
    pallas_call x1, Pallas kernels, fused_device(): pl.pallas_call(fused_kernel, out_shape=jax.ShapeDtypeStruct((half, out_wi...  116 us
    unnamed x1, local copies, waits for them, and re-layouts  2.7 us

commit v1 on v0

--- a/solution.py
+++ b/solution.py
@@ -76,7 +76,7 @@
 
 def fused_kernel(
     q_ref, k_ref, v_ref, doc_ref, w_hbm, out_ref,
-    kv, docs, q_wide, k_wide, v_wide, m_s, acc, att, w_vm, part, theirs, swapped,
+    kv, docs, flags, q_wide, k_wide, v_wide, m_s, acc, att, w_vm, total, theirs, swapped,
     send_sem, recv_sem, dsend_sem, drecv_sem, w_sem, osend_sem, orecv_sem,
 ):
     tok = q_ref.shape[0]
@@ -168,7 +168,7 @@
         forward(jnp.int32(0), h)
         return carry
 
-    lax.fori_loop(0, heads, send_own, 0)
+    lax.fori_loop(0, 2, send_own, 0)
 
     score_scale = HEAD_WIDTH ** (-0.5) * LOG2E
     doc_rows = lax.broadcasted_iota(jnp.int32, (HEAD_WIDTH, tok), 0)
@@ -178,26 +178,26 @@
         return flags.T.astype(jnp.bfloat16)
 
     own_docs = doc_columns(0, 1.0, 0.0)
-    for head in range(heads * group):
-        q_wide[head, :, :HEAD_WIDTH] = q_ref[:, head * HEAD_WIDTH:(head + 1) * HEAD_WIDTH]
-        q_wide[head, :, HEAD_WIDTH:] = own_docs
+    for r in range(group):
+        q_wide[r, :, HEAD_WIDTH:] = own_docs
     v_wide[:, HEAD_WIDTH:] = jnp.ones((v_wide.shape[0], HEAD_WIDTH), jnp.bfloat16)
 
     def fill(j, s, h):
-        k_wide[j * tok:(j + 1) * tok, :HEAD_WIDTH] = kv[s, h, 0]
-        v_wide[j * tok:(j + 1) * tok, :HEAD_WIDTH] = kv[s, h, 1]
-
         @pl.when(h == 0)
         def _():
-            k_wide[j * tok:(j + 1) * tok, HEAD_WIDTH:] = doc_columns(s, 0.0, NEG)
-
-    def piece(h, count, first):
+            flags[s] = doc_columns(s, 0.0, NEG)
+
+        k_wide[j * tok:(j + 1) * tok, :HEAD_WIDTH] = kv[s, h, 0]
+        k_wide[j * tok:(j + 1) * tok, HEAD_WIDTH:] = flags[s]
+        v_wide[j * tok:(j + 1) * tok, :HEAD_WIDTH] = kv[s, h, 1]
+
+    def piece(count, first):
         keys = k_wide[:count]
         values = v_wide[:count]
 
         def score(r):
             return lax.dot_general(
-                q_wide[h * group + r], keys, (((1,), (1,)), ((), ())),
+                q_wide[r], keys, (((1,), (1,)), ((), ())),
                 preferred_element_type=jnp.float32,
             )
 
@@ -206,7 +206,6 @@
             scores = upcoming
             if r + 1 < group:
                 upcoming = score(r + 1)
-            head = h * group + r
             if first:
                 rows = lax.broadcasted_iota(jnp.int32, (tok, tok), 0)
                 cols = lax.broadcasted_iota(jnp.int32, (tok, tok), 1)
@@ -215,23 +214,16 @@
                 jnp.max(scores, axis=1, keepdims=True), (tok, HEAD_WIDTH)
             )
             if not first:
-                before = m_s[head]
+                before = m_s[r]
                 top = jnp.maximum(before, top)
             shift = jnp.concatenate([top * score_scale] * (count // HEAD_WIDTH), axis=1)
             weights = jnp.exp2(scores * score_scale - shift).astype(jnp.bfloat16)
             summed = jnp.dot(weights, values, preferred_element_type=jnp.float32)
             if not first:
                 fade = jnp.exp2((before - top) * score_scale)
-                summed = summed + acc[head] * jnp.concatenate([fade, fade], axis=1)
-            m_s[head] = top
-            acc[head] = summed
-
-    def own_piece(h, carry):
-        fill(0, 0, h)
-        piece(h, tok, True)
-        return carry
-
-    lax.fori_loop(0, heads, own_piece, 0)
+                summed = summed + acc[r] * jnp.concatenate([fade, fade], axis=1)
+            m_s[r] = top
+            acc[r] = summed
 
     turn = 3
     x_third = x * (7 - 4 * y) + (1 - x)
@@ -248,42 +240,14 @@
         third = jnp.where(late, z_slot, y_slot)
         return jnp.where(j == 0, first, jnp.where(j == 1, second, third))
 
-    def arrive(t, carry):
-        around = t // heads
-        h = t % heads
-        for j in range(turn):
-            s = pick(around * turn + j)
-
-            @pl.when(me >= s)
-            def _():
-                pltpu.make_async_copy(kv.at[s, h], kv.at[s, h], recv_sem.at[s, h]).wait()
-
-                @pl.when(h == 0)
-                def _():
-                    pltpu.make_async_copy(docs.at[s], docs.at[s], drecv_sem.at[s]).wait()
-
-                forward(s, h)
-
-        for j in range(turn):
-            fill(j, pick(around * turn + j), h)
-        piece(h, turn * tok, False)
-        return carry
-
-    lax.fori_loop(0, REACH // turn * heads, arrive, 0)
-
-    def finish(head, carry):
-        att[:, pl.ds(pl.multiple_of(head * HEAD_WIDTH, HEAD_WIDTH), HEAD_WIDTH)] = (
-            acc[head, :, :HEAD_WIDTH] / acc[head, :, HEAD_WIDTH:]
-        ).astype(jnp.bfloat16)
-        return carry
-
-    lax.fori_loop(0, heads * group, finish, 0)
-    weight_copy.wait()
-
     half = out_ref.shape[0]
     tiles = out_ref.shape[1] // OUT_TILE
     keep = pl.multiple_of(core * half, half)
     give = pl.multiple_of((1 - core) * half, half)
+    span = group * HEAD_WIDTH
+
+    def tile_columns(i):
+        return pl.ds(pl.multiple_of(i * OUT_TILE, OUT_TILE), OUT_TILE)
 
     def swap_copy(i):
         return pltpu.make_async_remote_copy(
@@ -294,21 +258,80 @@
             device_id={"head": 1 - core},
         )
 
-    def project(i, carry):
-        columns = pl.ds(pl.multiple_of(i * OUT_TILE, OUT_TILE), OUT_TILE)
-        part[...] = jnp.dot(att[...], w_vm[:, columns], preferred_element_type=jnp.float32)
-        theirs[i] = part[pl.ds(give, half), :].astype(jnp.bfloat16)
-        swap_copy(i).start()
-        out_ref[:, columns] = part[pl.ds(keep, half), :].astype(jnp.bfloat16)
+    def one_head(h, carry):
+        @pl.when((h >= 1) & (h < heads - 1))
+        def _():
+            forward(jnp.int32(0), h + 1)
+
+        for r in range(group):
+            place = pl.multiple_of(h * span + r * HEAD_WIDTH, HEAD_WIDTH)
+            q_wide[r, :, :HEAD_WIDTH] = q_ref[:, pl.ds(place, HEAD_WIDTH)]
+        fill(0, 0, h)
+        piece(tok, True)
+
+        def arrive(around, inner):
+            for j in range(turn):
+                s = pick(around * turn + j)
+
+                @pl.when(me >= s)
+                def _():
+                    pltpu.make_async_copy(kv.at[s, h], kv.at[s, h], recv_sem.at[s, h]).wait()
+
+                    @pl.when(h == 0)
+                    def _():
+                        pltpu.make_async_copy(docs.at[s], docs.at[s], drecv_sem.at[s]).wait()
+
+                    forward(s, h)
+
+            for j in range(turn):
+                fill(j, pick(around * turn + j), h)
+            piece(turn * tok, False)
+            return inner
+
+        lax.fori_loop(0, REACH // turn, arrive, 0)
+
+        for r in range(group):
+            att[:, r * HEAD_WIDTH:(r + 1) * HEAD_WIDTH] = (
+                acc[r, :, :HEAD_WIDTH] / acc[r, :, HEAD_WIDTH:]
+            ).astype(jnp.bfloat16)
+
+        @pl.when(h == 0)
+        def _():
+            weight_copy.wait()
+
+        weight_rows = pl.ds(pl.multiple_of(h * span, span), span)
+
+        def project(i, inner):
+            columns = tile_columns(i)
+            share = jnp.dot(
+                att[...], w_vm[weight_rows, columns], preferred_element_type=jnp.float32
+            )
+
+            @pl.when(h == 0)
+            def _():
+                total[:, columns] = share
+
+            @pl.when(h > 0)
+            def _():
+                total[:, columns] += share
+
+            @pl.when(h == heads - 1)
+            def _():
+                theirs[i] = total[pl.ds(give, half), columns].astype(jnp.bfloat16)
+                swap_copy(i).start()
+
+            return inner
+
+        lax.fori_loop(0, tiles, project, 0)
         return carry
 
-    lax.fori_loop(0, tiles, project, 0)
+    lax.fori_loop(0, heads, one_head, 0)
 
     def combine(i, carry):
         swap_copy(i).wait()
-        columns = pl.ds(pl.multiple_of(i * OUT_TILE, OUT_TILE), OUT_TILE)
+        columns = tile_columns(i)
         out_ref[:, columns] = (
-            out_ref[:, columns].astype(jnp.float32) + swapped[i].astype(jnp.float32)
+            total[pl.ds(keep, half), columns] + swapped[i].astype(jnp.float32)
         ).astype(jnp.bfloat16)
         return carry
 
@@ -329,7 +352,7 @@
 def fused_device(queries, key_matrix, value_matrix, doc_ids, out_weight):
     tok, width = queries.shape
     heads = key_matrix.shape[1] // HEAD_WIDTH
-    query_heads = width // HEAD_WIDTH
+    group = width // key_matrix.shape[1]
     out_width = out_weight.shape[1]
     half = tok // 2
     tiles = out_width // OUT_TILE
@@ -343,14 +366,15 @@
         scratch_shapes=[
             pltpu.VMEM((SLOTS, heads, 2, tok, HEAD_WIDTH), bf16),
             pltpu.VMEM((SLOTS, 8, tok), jnp.int32),
-            pltpu.VMEM((query_heads, tok, 2 * HEAD_WIDTH), bf16),
+            pltpu.VMEM((SLOTS, tok, HEAD_WIDTH), bf16),
+            pltpu.VMEM((group, tok, 2 * HEAD_WIDTH), bf16),
             pltpu.VMEM((3 * tok, 2 * HEAD_WIDTH), bf16),
             pltpu.VMEM((3 * tok, 2 * HEAD_WIDTH), bf16),
-            pltpu.VMEM((query_heads, tok, HEAD_WIDTH), f32),
-            pltpu.VMEM((query_heads, tok, 2 * HEAD_WIDTH), f32),
-            pltpu.VMEM((tok, width), bf16),
+            pltpu.VMEM((group, tok, HEAD_WIDTH), f32),
+            pltpu.VMEM((group, tok, 2 * HEAD_WIDTH), f32),
+            pltpu.VMEM((tok, group * HEAD_WIDTH), bf16),
             pltpu.VMEM(out_weight.shape, bf16),
-            pltpu.VMEM((tok, OUT_TILE), f32),
+            pltpu.VMEM((tok, out_width), f32),
             pltpu.VMEM((tiles, half, OUT_TILE), bf16),
             pltpu.VMEM((tiles, half, OUT_TILE), bf16),
             pltpu.SemaphoreType.DMA((3, SLOTS, heads)),
@@ -364,7 +388,7 @@
         compiler_params=pltpu.CompilerParams(
             collective_id=0, has_side_effects=True, vmem_limit_bytes=58 * 1024 * 1024
         ),
-    )(queries, key_matrix, value_matrix, doc_ids[None, :], out_weight)
+    )(queries, key_matrix, value_matrix, doc_ids.reshape(1, tok), out_weight)
 
 
 def solution(mesh):

time: 120 us -> 119 us (level)
  Pallas kernels: 116 us -> 114 us
    pallas_call x1, Pallas kernels: 116 us -> 114 us  [fused_device(): pl.pallas_call(fused_kernel, out_shape=jax.ShapeDtypeStruct((half, out_wi...]
    broadcast_in_dim x1 -> x0, local copies, waits for them, and re-layouts: 1.24 us -> none  [fused_device(): doc_ids[None, :]]
    reshape x0 -> x1, local copies, waits for them, and re-layouts: none -> 1.24 us  [fused_device(): doc_ids.reshape(1, tok)]
where the time goes in v1:
time: 119 us; the launch traced here: 118 us
  Pallas kernels  114 us (96%)
  local copies, waits for them, and re-layouts  3.95 us (3%)
    pallas_call x1, Pallas kernels, fused_device(): pl.pallas_call(fused_kernel, out_shape=jax.ShapeDtypeStruct((half, out_wi...  114 us
    unnamed x1, local copies, waits for them, and re-layouts  2.7 us

profile of v1, /device:TPU:25, one launch (start us, length us, event | category | flops | bytes accessed | tf_op | source)
XLA Modules:
  0.0 117.6 jit_solution(16641653327748829043)
XLA Ops:
  0.0 1.2 %reshape.3.doc_ref = s32[1,384]{1,0:T(1,128)} reshape(s32[384]{0:T(512)} %param.8) | data formatting | bytes 3072 | tf_op jit(solution)/shard_map/reshape | solution.py:391
  1.2 113.7 %shard_map.55 = bf16[192,4096]{1,0:T(8,128)(2,1)} custom-call(bf16[384,2048]{1,0:T(8,128)(2,1)} %q_ref.1, bf16[384,512]{1,0:T(8,128)(2,1)} %k_ref.1, bf16[384,512]{1,0:T(8,128)(2,1)} %v_ref.1, s32[1,384]{1,0:T(1,128)} %reshape.3.doc_ref, bf16[2048,4096]{1,0:T(8,128)(2,1)} %w_hbm.1), custom_call_target="tpu_custom_call" | custom-call | tf_op jit(solution)/shard_map/pallas_call | solution.py:361
  114.9 2.7 %copy.7 = bf16[192,4096]{1,0:T(8,128)(2,1)} copy(bf16[192,4096]{1,0:T(8,128)(2,1)} %shard_map.55) | data formatting | bytes 3145728

commit v2 on v1

--- a/solution.py
+++ b/solution.py
@@ -147,28 +147,41 @@
             device_id={"ctx": me + step},
         )
 
-    def sends(link, s):
+    def sends(link, s, count=3):
         sources, _, also = links[link]
-        here = (s == sources[0]) | (s == sources[1]) | (s == sources[2])
+        here = s == sources[0]
+        for i in range(1, count):
+            here = here | (s == sources[i])
         if also is not None:
             here = here & also
         return here
 
+    def start_send(link, s, h):
+        @pl.when(h == 0)
+        def _():
+            doc_copy(link, s).start()
+
+        chunk_copy(link, s, h).start()
+
     def forward(s, h):
-        for link in (2, 0, 1):
-            @pl.when(sends(link, s))
-            def _():
-                @pl.when(h == 0)
-                def _():
-                    doc_copy(link, s).start()
-
-                chunk_copy(link, s, h).start()
+        for link, count in ((2, 3), (0, 2), (1, 2)):
+            @pl.when(sends(link, s, count))
+            def _():
+                start_send(link, s, h)
+
+    def forward_last(h):
+        for link in (0, 1):
+            s = links[link][0][2]
+
+            @pl.when(me >= s)
+            def _():
+                start_send(link, s, h)
 
     def send_own(h, carry):
         forward(jnp.int32(0), h)
         return carry
 
-    lax.fori_loop(0, 2, send_own, 0)
+    lax.fori_loop(0, heads, send_own, 0)
 
     score_scale = HEAD_WIDTH ** (-0.5) * LOG2E
     doc_rows = lax.broadcasted_iota(jnp.int32, (HEAD_WIDTH, tok), 0)
@@ -191,7 +204,10 @@
         k_wide[j * tok:(j + 1) * tok, HEAD_WIDTH:] = flags[s]
         v_wide[j * tok:(j + 1) * tok, :HEAD_WIDTH] = kv[s, h, 1]
 
-    def piece(count, first):
+    def piece(h, count, first):
+        for r in range(group):
+            place = pl.multiple_of((h * group + r) * HEAD_WIDTH, HEAD_WIDTH)
+            q_wide[r, :, :HEAD_WIDTH] = q_ref[:, pl.ds(place, HEAD_WIDTH)]
         keys = k_wide[:count]
         values = v_wide[:count]
 
@@ -204,6 +220,7 @@
         upcoming = score(0)
         for r in range(group):
             scores = upcoming
+            head = h * group + r
             if r + 1 < group:
                 upcoming = score(r + 1)
             if first:
@@ -214,16 +231,16 @@
                 jnp.max(scores, axis=1, keepdims=True), (tok, HEAD_WIDTH)
             )
             if not first:
-                before = m_s[r]
+                before = m_s[head]
                 top = jnp.maximum(before, top)
             shift = jnp.concatenate([top * score_scale] * (count // HEAD_WIDTH), axis=1)
             weights = jnp.exp2(scores * score_scale - shift).astype(jnp.bfloat16)
             summed = jnp.dot(weights, values, preferred_element_type=jnp.float32)
             if not first:
                 fade = jnp.exp2((before - top) * score_scale)
-                summed = summed + acc[r] * jnp.concatenate([fade, fade], axis=1)
-            m_s[r] = top
-            acc[r] = summed
+                summed = summed + acc[head] * jnp.concatenate([fade, fade], axis=1)
+            m_s[head] = top
+            acc[head] = summed
 
     turn = 3
     x_third = x * (7 - 4 * y) + (1 - x)
@@ -258,41 +275,11 @@
             device_id={"head": 1 - core},
         )
 
-    def one_head(h, carry):
-        @pl.when((h >= 1) & (h < heads - 1))
-        def _():
-            forward(jnp.int32(0), h + 1)
-
+    def project_head(h):
         for r in range(group):
-            place = pl.multiple_of(h * span + r * HEAD_WIDTH, HEAD_WIDTH)
-            q_wide[r, :, :HEAD_WIDTH] = q_ref[:, pl.ds(place, HEAD_WIDTH)]
-        fill(0, 0, h)
-        piece(tok, True)
-
-        def arrive(around, inner):
-            for j in range(turn):
-                s = pick(around * turn + j)
-
-                @pl.when(me >= s)
-                def _():
-                    pltpu.make_async_copy(kv.at[s, h], kv.at[s, h], recv_sem.at[s, h]).wait()
-
-                    @pl.when(h == 0)
-                    def _():
-                        pltpu.make_async_copy(docs.at[s], docs.at[s], drecv_sem.at[s]).wait()
-
-                    forward(s, h)
-
-            for j in range(turn):
-                fill(j, pick(around * turn + j), h)
-            piece(turn * tok, False)
-            return inner
-
-        lax.fori_loop(0, REACH // turn, arrive, 0)
-
-        for r in range(group):
+            head = h * group + r
             att[:, r * HEAD_WIDTH:(r + 1) * HEAD_WIDTH] = (
-                acc[r, :, :HEAD_WIDTH] / acc[r, :, HEAD_WIDTH:]
+                acc[head, :, :HEAD_WIDTH] / acc[head, :, HEAD_WIDTH:]
             ).astype(jnp.bfloat16)
 
         @pl.when(h == 0)
@@ -323,9 +310,47 @@
             return inner
 
         lax.fori_loop(0, tiles, project, 0)
-        return carry
-
-    lax.fori_loop(0, heads, one_head, 0)
+
+    def own_piece(h, carry):
+        fill(0, 0, h)
+        piece(h, tok, True)
+        return carry
+
+    lax.fori_loop(0, heads, own_piece, 0)
+    lag = heads + 2
+
+    def arrive(t, carry):
+        around = t // heads
+        h = t % heads
+
+        @pl.when((t >= lag) & (t < lag + heads))
+        def _():
+            forward_last(t - lag)
+
+        for j in range(turn):
+            s = pick(around * turn + j)
+
+            @pl.when(me >= s)
+            def _():
+                pltpu.make_async_copy(kv.at[s, h], kv.at[s, h], recv_sem.at[s, h]).wait()
+
+                @pl.when(h == 0)
+                def _():
+                    pltpu.make_async_copy(docs.at[s], docs.at[s], drecv_sem.at[s]).wait()
+
+                forward(s, h)
+
+        for j in range(turn):
+            fill(j, pick(around * turn + j), h)
+        piece(h, turn * tok, False)
+
+        @pl.when(around == REACH // turn - 1)
+        def _():
+            project_head(h)
+
+        return carry
+
+    lax.fori_loop(0, REACH // turn * heads, arrive, 0)
 
     def combine(i, carry):
         swap_copy(i).wait()
@@ -370,8 +395,8 @@
             pltpu.VMEM((group, tok, 2 * HEAD_WIDTH), bf16),
             pltpu.VMEM((3 * tok, 2 * HEAD_WIDTH), bf16),
             pltpu.VMEM((3 * tok, 2 * HEAD_WIDTH), bf16),
-            pltpu.VMEM((group, tok, HEAD_WIDTH), f32),
-            pltpu.VMEM((group, tok, 2 * HEAD_WIDTH), f32),
+            pltpu.VMEM((heads * group, tok, HEAD_WIDTH), f32),
+            pltpu.VMEM((heads * group, tok, 2 * HEAD_WIDTH), f32),
             pltpu.VMEM((tok, group * HEAD_WIDTH), bf16),
             pltpu.VMEM(out_weight.shape, bf16),
             pltpu.VMEM((tok, out_width), f32),
@@ -386,7 +411,7 @@
             pltpu.SemaphoreType.DMA((tiles,)),
         ],
         compiler_params=pltpu.CompilerParams(
-            collective_id=0, has_side_effects=True, vmem_limit_bytes=58 * 1024 * 1024
+            collective_id=0, has_side_effects=True, vmem_limit_bytes=60 * 1024 * 1024
         ),
     )(queries, key_matrix, value_matrix, doc_ids.reshape(1, tok), out_weight)
 

time: 119 us -> 105 us (0.88); the launches traced: 118 us -> 105 us
  Pallas kernels: 114 us -> 101 us
    pallas_call x1, Pallas kernels: 114 us -> 101 us  [fused_device(): pl.pallas_call(fused_kernel, out_shape=jax.ShapeDtypeStruct((half, out_wi...]
where the time goes in v2:
time: 105 us
  Pallas kernels  101 us (96%)
  local copies, waits for them, and re-layouts  3.95 us (4%)
    pallas_call x1, Pallas kernels, fused_device(): pl.pallas_call(fused_kernel, out_shape=jax.ShapeDtypeStruct((half, out_wi...  101 us
    unnamed x1, local copies, waits for them, and re-layouts  2.7 us

profile of v2, /device:TPU:25, one launch (start us, length us, event | category | flops | bytes accessed | tf_op | source)
XLA Modules:
  0.0 104.9 jit_solution(12626855529091236172)
XLA Ops:
  0.0 1.2 %reshape.3.doc_ref = s32[1,384]{1,0:T(1,128)} reshape(s32[384]{0:T(512)} %param.8) | data formatting | bytes 3072 | tf_op jit(solution)/shard_map/reshape | solution.py:416
  1.2 101.0 %shard_map.55 = bf16[192,4096]{1,0:T(8,128)(2,1)} custom-call(bf16[384,2048]{1,0:T(8,128)(2,1)} %q_ref.1, bf16[384,512]{1,0:T(8,128)(2,1)} %k_ref.1, bf16[384,512]{1,0:T(8,128)(2,1)} %v_ref.1, s32[1,384]{1,0:T(1,128)} %reshape.3.doc_ref, bf16[2048,4096]{1,0:T(8,128)(2,1)} %w_hbm.1), custom_call_target="tpu_custom_call" | custom-call | tf_op jit(solution)/shard_map/pallas_call | solution.py:386
  102.2 2.7 %copy.7 = bf16[192,4096]{1,0:T(8,128)(2,1)} copy(bf16[192,4096]{1,0:T(8,128)(2,1)} %shard_map.55) | data formatting | bytes 3145728

commit v3 on v2

--- a/solution.py
+++ b/solution.py
@@ -117,23 +117,17 @@
         kv[0, h, 1] = v_ref[:, columns]
     docs[0] = jnp.broadcast_to(doc_ref[...], docs.shape[1:])
 
-    def blank(s, carry):
-        docs[s] = jnp.full(docs.shape[1:], -1, jnp.int32)
-        kv[s] = jnp.zeros(kv.shape[1:], kv.dtype)
-        return carry
-
-    lax.fori_loop(jnp.minimum(me + 1, SLOTS), SLOTS, blank, 0)
 
     peers = 3 + jnp.where(z > 0, 1, 0) + jnp.where(z < planes - 1, 1, 0)
     pl.semaphore_wait(barrier, peers)
 
-    def chunk_copy(link, s, h):
+    def chunk_copy(link, s, h, half):
         step = links[link][1]
         return pltpu.make_async_remote_copy(
-            src_ref=kv.at[s, h],
-            dst_ref=kv.at[s + step, h],
-            send_sem=send_sem.at[link, s, h],
-            recv_sem=recv_sem.at[s + step, h],
+            src_ref=kv.at[s, h, half],
+            dst_ref=kv.at[s + step, h, half],
+            send_sem=send_sem.at[link, s, h, half],
+            recv_sem=recv_sem.at[s + step, h, half],
             device_id={"ctx": me + step},
         )
 
@@ -156,18 +150,19 @@
             here = here & also
         return here
 
-    def start_send(link, s, h):
-        @pl.when(h == 0)
-        def _():
-            doc_copy(link, s).start()
-
-        chunk_copy(link, s, h).start()
-
-    def forward(s, h):
+    def start_send(link, s, h, half):
+        if half == 0:
+            @pl.when(h == 0)
+            def _():
+                doc_copy(link, s).start()
+
+        chunk_copy(link, s, h, half).start()
+
+    def forward(s, h, half):
         for link, count in ((2, 3), (0, 2), (1, 2)):
             @pl.when(sends(link, s, count))
             def _():
-                start_send(link, s, h)
+                start_send(link, s, h, half)
 
     def forward_last(h):
         for link in (0, 1):
@@ -175,13 +170,22 @@
 
             @pl.when(me >= s)
             def _():
-                start_send(link, s, h)
+                start_send(link, s, h, 0)
+                start_send(link, s, h, 1)
 
     def send_own(h, carry):
-        forward(jnp.int32(0), h)
+        forward(jnp.int32(0), h, 0)
+        forward(jnp.int32(0), h, 1)
         return carry
 
     lax.fori_loop(0, heads, send_own, 0)
+
+    def blank(s, carry):
+        docs[s] = jnp.full(docs.shape[1:], -1, jnp.int32)
+        kv[s] = jnp.zeros(kv.shape[1:], kv.dtype)
+        return carry
+
+    lax.fori_loop(jnp.minimum(me + 1, SLOTS), SLOTS, blank, 0)
 
     score_scale = HEAD_WIDTH ** (-0.5) * LOG2E
     doc_rows = lax.broadcasted_iota(jnp.int32, (HEAD_WIDTH, tok), 0)
@@ -311,12 +315,11 @@
 
         lax.fori_loop(0, tiles, project, 0)
 
-    def own_piece(h, carry):
+    def own_piece(h):
         fill(0, 0, h)
         piece(h, tok, True)
-        return carry
-
-    lax.fori_loop(0, heads, own_piece, 0)
+
+    own_piece(jnp.int32(0))
     lag = heads + 2
 
     def arrive(t, carry):
@@ -327,18 +330,26 @@
         def _():
             forward_last(t - lag)
 
-        for j in range(turn):
-            s = pick(around * turn + j)
-
-            @pl.when(me >= s)
-            def _():
-                pltpu.make_async_copy(kv.at[s, h], kv.at[s, h], recv_sem.at[s, h]).wait()
-
-                @pl.when(h == 0)
+        for half in range(2):
+            for j in range(turn):
+                s = pick(around * turn + j)
+
+                @pl.when(me >= s)
                 def _():
-                    pltpu.make_async_copy(docs.at[s], docs.at[s], drecv_sem.at[s]).wait()
-
-                forward(s, h)
+                    landed = kv.at[s, h, half]
+                    pltpu.make_async_copy(landed, landed, recv_sem.at[s, h, half]).wait()
+                    if half == 0:
+                        @pl.when(h == 0)
+                        def _():
+                            pltpu.make_async_copy(
+                                docs.at[s], docs.at[s], drecv_sem.at[s]
+                            ).wait()
+
+                    forward(s, h, half)
+
+        @pl.when(t < heads - 1)
+        def _():
+            own_piece(t + 1)
 
         for j in range(turn):
             fill(j, pick(around * turn + j), h)
@@ -368,7 +379,8 @@
             def _():
                 doc_copy(link, s).wait_send()
                 for h in range(heads):
-                    chunk_copy(link, s, h).wait_send()
+                    for half in range(2):
+                        chunk_copy(link, s, h, half).wait_send()
         return carry
 
     lax.fori_loop(0, SLOTS, settle, 0)
@@ -402,8 +414,8 @@
             pltpu.VMEM((tok, out_width), f32),
             pltpu.VMEM((tiles, half, OUT_TILE), bf16),
             pltpu.VMEM((tiles, half, OUT_TILE), bf16),
-            pltpu.SemaphoreType.DMA((3, SLOTS, heads)),
-            pltpu.SemaphoreType.DMA((SLOTS, heads)),
+            pltpu.SemaphoreType.DMA((3, SLOTS, heads, 2)),
+            pltpu.SemaphoreType.DMA((SLOTS, heads, 2)),
             pltpu.SemaphoreType.DMA((3, SLOTS)),
             pltpu.SemaphoreType.DMA((SLOTS,)),
             pltpu.SemaphoreType.DMA,

time: 105 us -> 109 us (1.038)
  Pallas kernels: 101 us -> 105 us
    pallas_call x1, Pallas kernels: 101 us -> 105 us  [fused_device(): pl.pallas_call(fused_kernel, out_shape=jax.ShapeDtypeStruct((half, out_wi...]
where the time goes in v3:
time: 109 us
  Pallas kernels  105 us (96%)
  local copies, waits for them, and re-layouts  3.95 us (4%)
    pallas_call x1, Pallas kernels, fused_device(): pl.pallas_call(fused_kernel, out_shape=jax.ShapeDtypeStruct((half, out_wi...  105 us
    unnamed x1, local copies, waits for them, and re-layouts  2.7 us

profile of v3, /device:TPU:25, one launch (start us, length us, event | category | flops | bytes accessed | tf_op | source)
XLA Modules:
  0.0 108.6 jit_solution(2918130937462227820)
XLA Ops:
  0.0 1.2 %reshape.3.doc_ref = s32[1,384]{1,0:T(1,128)} reshape(s32[384]{0:T(512)} %param.8) | data formatting | bytes 3072 | tf_op jit(solution)/shard_map/reshape | solution.py:428
  1.2 104.6 %shard_map.55 = bf16[192,4096]{1,0:T(8,128)(2,1)} custom-call(bf16[384,2048]{1,0:T(8,128)(2,1)} %q_ref.1, bf16[384,512]{1,0:T(8,128)(2,1)} %k_ref.1, bf16[384,512]{1,0:T(8,128)(2,1)} %v_ref.1, s32[1,384]{1,0:T(1,128)} %reshape.3.doc_ref, bf16[2048,4096]{1,0:T(8,128)(2,1)} %w_hbm.1), custom_call_target="tpu_custom_call" | custom-call | tf_op jit(solution)/shard_map/pallas_call | solution.py:398
  105.9 2.7 %copy.7 = bf16[192,4096]{1,0:T(8,128)(2,1)} copy(bf16[192,4096]{1,0:T(8,128)(2,1)} %shard_map.55) | data formatting | bytes 3145728
